TPU v7x, 512 devices: a whole 4x8x8 slice. The times are simulated.
512 devices in a mesh: tm: 8 (over z_hi, core), particle: 8 (over y), cell: 8 (over x, z_lo).
Axes of the slice: x: 4, y: 8, z: 8 (z_hi: 4, z_lo: 2; z = z_hi * 2 + z_lo), core: 2. Of those that a mesh axis runs over, the one named last changes fastest.
Arguments:
- particles: float32 [8, 30, 8192], P('tm', None, 'particle'), may hold values from -50 to 50
- cell_points: float32 [8, 30, 8192], P('tm', None, 'cell'), may hold values from -50 to 50
- cell_counts: int32 [8], replicated, may hold values from 1365 to 8192, as said below
- brownian: float32 [8, 30, 8192], P('tm', None, ('particle', 'cell')), may hold values from -6 to 6
Outputs:
- descent_direction: float32 [8, 30, 8192], P('tm', None, ('particle', 'cell'))
- updated_particles: float32 [8, 30, 8192], P('tm', None, ('particle', 'cell'))
Inputs may be any that keep to these rules, and one draw needn't show every extreme that they name: `cell_counts`: some time has all 8192 cells observed.
All inputs are finite; a program needn't handle non-finite values.
Results may differ from a plain program's by a relative error of at most 0.0003.
Values sent between devices are 32-bit elements; how exact they have to be, the bound alone decides.
A program may use at most 64 MiB of HBM per device.

v0:
```python
import math

import jax
import jax.numpy as jnp
from jax import lax
from jax.sharding import PartitionSpec as P

DATA_VAR = 2.0
BRIDGE_VAR = 1.5
LANGEVIN_STRIDE = 0.05
NOISE_LEVEL = 1.0
lowest_score = -1e30


def joined(x, axis, combine):
    everything = jax.tree.map(lambda part: lax.all_gather(part, axis), x)
    first = jax.tree.map(lambda part: part[0], everything)

    def turn(k, so_far):
        return combine(so_far, jax.tree.map(lambda part: part[k], everything))

    return lax.fori_loop(1, lax.axis_size(axis), turn, first)


def passed_along(x, axis, by):
    count = lax.axis_size(axis)
    pairs = [(i, i + by) for i in range(count) if 0 <= i + by < count]
    return lax.ppermute(x, axis, pairs)


def fresh_state(feature_count, row_count):
    return (
        jnp.full((row_count,), lowest_score, jnp.float32),
        jnp.zeros((row_count,), jnp.float32),
        jnp.zeros((feature_count, row_count), jnp.float32),
    )


def fold_targets(running, queries, query_sq, targets, usable, spread):
    highest_seen, summed, weighted = running
    cross_terms = lax.dot_general(
        queries,
        targets,
        (((0,), (0,)), ((), ())),
        precision=lax.Precision.HIGHEST,
        preferred_element_type=jnp.float32,
    )
    scores = (2.0 * cross_terms - query_sq[:, None] - jnp.sum(targets * targets, 0)[None, :]) / (
        2.0 * spread
    )
    scores = jnp.where(usable[None, :], scores, lowest_score)
    new_high = jnp.maximum(highest_seen, jnp.max(scores, 1))
    factor = jnp.exp(highest_seen - new_high)
    expo_terms = jnp.where(usable[None, :], jnp.exp(scores - new_high[:, None]), 0.0)
    summed = summed * factor + jnp.sum(expo_terms, 1)
    weighted = weighted * factor[None, :] + lax.dot_general(
        targets,
        expo_terms,
        (((1,), (1,)), ((), ())),
        precision=lax.Precision.HIGHEST,
        preferred_element_type=jnp.float32,
    )
    return (new_high, summed, weighted)


def sweep(running, queries, query_sq, targets, spread, first_key, key_limit):
    key_span = math.gcd(targets.shape[1], 512)
    key_rounds = targets.shape[1] // key_span

    def visit(turn_index, carried):
        offset = turn_index * key_span
        key_block = lax.dynamic_slice_in_dim(targets, offset, key_span, 1)
        usable = first_key + offset + jnp.arange(key_span, dtype=jnp.int32) < key_limit
        return fold_targets(carried, queries, query_sq, key_block, usable, spread)

    return lax.fori_loop(0, key_rounds, visit, running)


def combine_parts(earlier_part, later_part):
    new_high = jnp.maximum(earlier_part[0], later_part[0])
    scale_first = jnp.exp(earlier_part[0] - new_high)
    scale_second = jnp.exp(later_part[0] - new_high)
    summed = earlier_part[1] * scale_first + later_part[1] * scale_second
    weighted = earlier_part[2] * scale_first[None, :] + later_part[2] * scale_second[None, :]
    return (new_high, summed, weighted)


def shards(particles, cell_points, cell_counts, brownian):
    own_block = particles[0]
    own_cells = cell_points[0]
    feature_count = own_block.shape[0]
    block_rows = own_block.shape[1]
    share_width = block_rows // lax.axis_size("cell")
    cell_index = lax.axis_index("cell")
    time_index = lax.axis_index("tm")
    share_start = cell_index * share_width
    local_portion = lax.dynamic_slice_in_dim(own_block, share_start, share_width, 1)
    cell_limit = jnp.sum(
        jnp.where(jnp.arange(cell_counts.shape[0], dtype=jnp.int32) == time_index, cell_counts, 0)
    )
    first_cell = cell_index * own_cells.shape[1]
    block_sq = jnp.sum(own_block * own_block, 0)
    starting = fresh_state(feature_count, block_rows)
    fit_state = sweep(starting, own_block, block_sq, own_cells, DATA_VAR, first_cell, cell_limit)
    fit_high, fit_sum, fit_weighted = joined(
        (fit_state[0], fit_state[1], fit_state[2]), "cell", combine_parts
    )
    share_sum = lax.dynamic_slice_in_dim(fit_sum, share_start, share_width, 0)
    share_weighted = lax.dynamic_slice_in_dim(fit_weighted, share_start, share_width, 1)
    fit_mean = share_weighted / share_sum[None, :]
    share_sq = jnp.sum(local_portion * local_portion, 0)
    share_start_state = fresh_state(feature_count, share_width)
    earlier = passed_along(local_portion, "tm", 1)
    following = passed_along(local_portion, "tm", -1)
    prior_piece = lax.all_gather(earlier, ("particle", "cell"), axis=1, tiled=True)
    later_piece = lax.all_gather(following, ("particle", "cell"), axis=1, tiled=True)
    prior_state = sweep(
        share_start_state, local_portion, share_sq, prior_piece, BRIDGE_VAR, 0, prior_piece.shape[1]
    )
    later_state = sweep(
        share_start_state, local_portion, share_sq, later_piece, BRIDGE_VAR, 0, later_piece.shape[1]
    )
    prior_mean = prior_state[2] / prior_state[1][None, :]
    later_mean = later_state[2] / later_state[1][None, :]
    has_prior = (time_index > 0).astype(jnp.float32)
    has_later = (time_index < lax.axis_size("tm") - 1).astype(jnp.float32)
    gradient = (local_portion - fit_mean) / DATA_VAR
    gradient = gradient + has_prior * (local_portion - prior_mean) / BRIDGE_VAR
    gradient = gradient + has_later * (local_portion - later_mean) / BRIDGE_VAR
    descent_direction = -gradient
    updated_particles = (
        local_portion
        + LANGEVIN_STRIDE * descent_direction
        + math.sqrt(2.0 * LANGEVIN_STRIDE * NOISE_LEVEL) * brownian[0]
    )
    return (descent_direction[None], updated_particles[None])


def solution(mesh):
    in_specs = (
        P("tm", None, "particle"),
        P("tm", None, "cell"),
        P(),
        P("tm", None, ("particle", "cell")),
    )
    out_specs = (P("tm", None, ("particle", "cell")), P("tm", None, ("particle", "cell")))
    return jax.shard_map(shards, mesh=mesh, in_specs=in_specs, out_specs=out_specs, check_vma=False)
```

profile of v0, /device:TPU:128, one launch (start us, length us, event | category | flops | bytes accessed | tf_op | source)
XLA Modules:
  0.0 495.2 jit_solution(1083620822759951898)
XLA Ops:
  2.0 1.9 collective-permute-start
  3.9 4.5 collective-permute-start.1
  12.5 9.7 %while.74 = (s32[]{:T(128)}, f32[1024]{0:T(1024)S(1)}, f32[1024]{0:T(1024)S(1)}, f32[30,1024]{1,0:T(8,128)S(1)}, s32[]{:T(128)}, /*index=5*/s32[]{:T(128)}, f32[...) while((s32[]{:T(128)}, f32[1024]{0:T(1024)S(1)}, ...), condition=%wide.region_6.7_spmd.clone, body=%wide.region_2.6_spmd.clone.sunk | while | flops 383383040 | bytes 6944983 | solution.py:76
  13.1 2.2 fusion.74
  15.8 1.6 fusion.77
  18.0 2.2 fusion.74
  20.6 1.6 fusion.77
  22.2 28.5 %all-gather = f32[8192]{0:T(1024)S(1)} all-gather(f32[1024]{0:T(1024)S(1)} %get-tuple-element.585), channel_id=2, replica_groups=mesh['tm'=8,'particle'=8,'cell'=8] {'cell'}, dimensions={0}, use_global_device_ids=true | all-gather | bytes 36864 | tf_op jit(solution)/shard_map/all_gather | solution.py:16
  50.8 28.1 %all-gather.1 = f32[8192]{0:T(1024)S(1)} all-gather(f32[1024]{0:T(1024)S(1)} %get-tuple-element.586), channel_id=3, replica_groups=mesh['tm'=8,'particle'=8,'cell'=8] {'cell'}, dimensions={0}, use_global_device_ids=true | all-gather | bytes 36864 | tf_op jit(solution)/shard_map/all_gather | solution.py:16
  78.9 32.9 %all-gather.3 = f32[8,30,1024]{2,1,0:T(8,128)S(1)} all-gather(f32[1,30,1024]{2,1,0:T(8,128)S(1)} %bitcast.44), channel_id=4, replica_groups=mesh['tm'=8,'particle'=8,'cell'=8] {'cell'}, dimensions={0}, use_global_device_ids=true | all-gather | bytes 1105920 | tf_op jit(solution)/shard_map/all_gather | solution.py:16
  112.8 161.8 %all_gather.30 = f32[30,8192]{1,0:T(8,128)S(1)} all-gather(f32[30,128]{1,0:T(8,128)S(1)} %collective-permute-done), channel_id=1, replica_groups=mesh['tm'=8,'particle'=8,'cell'=8] {'particle','cell'}, dimensions={1}, use_global_device_ids=true | all-gather | bytes 998400 | tf_op jit(solution)/shard_map/all_gather | solution.py:115
  274.5 31.9 %while.75 = (s32[]{:T(128)}, f32[128]{0:T(128)S(1)}, f32[128]{0:T(128)S(1)}, f32[30,128]{1,0:T(8,128)S(1)}, f32[30,8192]{1,0:T(8,128)S(1)}, /*index=5*/f32[30,12...) while((s32[]{:T(128)}, f32[128]{0:T(128)S(1)}, ...), condition=%wide.region_14.15_spmd.clone, body=%wide.region_10.14_spmd.clone.sunk | while | flops 47950212 | bytes 1041079 | solution.py:76
  274.6 1.4 fusion.80
  278.6 1.4 fusion.80
  280.6 1.4 fusion.80
  282.6 1.4 fusion.80
  284.5 1.4 fusion.80
  286.5 1.4 fusion.80
  290.5 1.4 fusion.80
  292.5 1.4 fusion.80
  294.5 1.4 fusion.80
  296.5 1.4 fusion.80
  306.4 155.6 %all_gather.31 = f32[30,8192]{1,0:T(8,128)S(1)} all-gather(f32[30,128]{1,0:T(8,128)S(1)} %collective-permute-done.1), channel_id=1, replica_groups=mesh['tm'=8,'particle'=8,'cell'=8] {'particle','cell'}, dimensions={1}, use_global_device_ids=true | all-gather | bytes 998400 | tf_op jit(solution)/shard_map/all_gather | solution.py:116
  462.1 31.9 %while.76 = (s32[]{:T(128)}, f32[128]{0:T(128)S(1)}, f32[128]{0:T(128)S(1)}, f32[30,128]{1,0:T(8,128)S(1)}, f32[30,8192]{1,0:T(8,128)S(1)}, /*index=5*/f32[30,12...) while((s32[]{:T(128)}, f32[128]{0:T(128)S(1)}, ...), condition=%wide.region_19.20_spmd.clone, body=%wide.region_15.19_spmd.clone.sunk | while | flops 47950212 | bytes 1041079 | solution.py:76
  (309 shorter events, 58.4 us)
Async XLA Ops:
  2.0 110.8 %collective-permute-start = (f32[30,128]{1,0:T(8,128)}, f32[30,128]{1,0:T(8,128)S(1)}, u32[]{:S(2)}, u32[]{:S(2)}) collective-permute-start(f32[30,128]{1,0:T(8,128)} %bitcast.31), channel_id=1, source_target_pairs={{0,64},{64,128},{128,192},{192,256},{256,320},{320,384},{384,448},... | collective-permute-start | bytes 46088 | tf_op jit(solution)/shard_map/ppermute | solution.py:28
  3.9 302.6 %collective-permute-start.1 = (f32[30,128]{1,0:T(8,128)}, f32[30,128]{1,0:T(8,128)S(1)}, u32[]{:S(2)}, u32[]{:S(2)}) collective-permute-start(f32[30,128]{1,0:T(8,128)} %bitcast.31), channel_id=1, source_target_pairs={{64,0},{128,64},{192,128},{256,192},{320,256},{384,320},{448,384},... | collective-permute-start | bytes 46088 | tf_op jit(solution)/shard_map/ppermute | solution.py:28
  462.1 31.9 %copy-start = (f32[1,30,128]{2,0,1:T(1,128)S(1)}, f32[1,30,128]{2,0,1:T(1,128)}, u32[]{:S(2)}) copy-start(f32[1,30,128]{2,0,1:T(1,128)} %param.15) | copy-start | bytes 46084
where the time goes:
time: 498 us; the launch traced here: 495 us
  blocking collectives  407 us (82%)
  matrix products  62.8 us (13%)
  other arithmetic  11.4 us (2%)
  starting transfers between devices  6.45 us (1%)
    all_gather x1, blocking collectives, shards(): lax.all_gather(earlier, ('particle', 'cell'), axis=1, tiled=True)  162 us
    all_gather x1, blocking collectives, shards(): lax.all_gather(following, ('particle', 'cell'), axis=1, tiled=True)  156 us
    all_gather x3, blocking collectives, joined(): everything = jax.tree.map(lambda part: lax.all_gather(part, axis), x)  89.5 us
    dot_general x34, matrix products, fold_targets(): lax.dot_general(queries, targets, (((0,), (0,)), ((), ())), precision=lax...  48.1 us
    dot_general x34, matrix products, fold_targets(): lax.dot_general(targets, expo_terms, (((1,), (1,)), ((), ())), precision=...  14.7 us
  transfers between devices with their start and end apart: 2, of which 0 were waited for; matrix products, arithmetic and copies ran while one was open for 9% of the time, Pallas kernels for 0%

commit v1 on v0

v1 whole, which is shorter than its diff:
```python
import functools
import math

import jax
import jax.numpy as jnp
from jax import lax
from jax.experimental import pallas as pl
from jax.experimental.pallas import tpu as pltpu
from jax.sharding import PartitionSpec as P

DATA_VAR = 2.0
BRIDGE_VAR = 1.5
LANGEVIN_STRIDE = 0.05
NOISE_LEVEL = 1.0
MASKED_SCORE = -1e30
LOG2E = math.log2(math.e)
MESH = pl.DeviceIdType.MESH
bf16, f32 = jnp.bfloat16, jnp.float32
ROWS = 32
CHUNK = 512


def split3(x):
    high = x.astype(bf16)
    rest = x - high.astype(f32)
    low = rest.astype(bf16)
    return high, low, (rest - low.astype(f32)).astype(bf16)


def query_stack(q):
    count = q.shape[1]
    ext = jnp.concatenate([q, jnp.ones((1, count), f32), jnp.zeros((1, count), f32)], 0)
    h, l, ll = split3(ext)
    return jnp.concatenate([h, h, l, l, h, ll], 0)


def target_stack(t, alpha, usable=None):
    count = t.shape[1]
    bias = -alpha * jnp.sum(t * t, 0, keepdims=True)
    if usable is not None:
        bias = jnp.where(usable, bias, MASKED_SCORE)
    ext = jnp.concatenate([t * (2.0 * alpha), bias, jnp.zeros((1, count), f32)], 0)
    h, l, ll = split3(ext)
    stack = jnp.concatenate([h, l, h, l, ll, h], 0)
    row = lax.broadcasted_iota(jnp.int32, ext.shape, 0)
    wh = jnp.where(row == 30, 1.0, h.astype(f32)).astype(bf16)
    wl = jnp.where(row == 30, 0.0, l.astype(f32)).astype(bf16)
    return stack, wh, wl


def kernel(
    sizes,
    counts, x_hbm, cells_hbm, noise_hbm,
    d_out, u_out,
    x_ref, cells_ref, noise_ref, near, queries, targets, scores, parts, got,
    in_sem, near_send, near_recv, part_send, part_recv,
):
    times, peers = sizes
    t, p, c = (lax.axis_index(a) for a in ("tm", "particle", "cell"))
    block = x_ref.shape[1]
    share = block // peers

    loads = [
        pltpu.make_async_copy(x_hbm.at[0], x_ref, in_sem.at[0]),
        pltpu.make_async_copy(cells_hbm.at[0], cells_ref, in_sem.at[1]),
        pltpu.make_async_copy(noise_hbm.at[0], noise_ref, in_sem.at[2]),
    ]
    for load in loads:
        load.start()

    after, before = lax.rem(t + 1, times), lax.rem(t + times - 1, times)
    others = [(after, c, p), (before, c, p)]
    mates = [(t, p, lax.rem(c + k, peers)) for k in range(1, peers)]
    barrier = pltpu.get_barrier_semaphore()
    for device in others + mates:
        pl.semaphore_signal(barrier, inc=1, device_id=device, device_id_type=MESH)
    pl.semaphore_wait(barrier, len(others) + len(mates))

    moves = [
        pltpu.make_async_remote_copy(
            src_ref=x_hbm.at[0], dst_ref=near.at[i],
            send_sem=near_send.at[i], recv_sem=near_recv.at[i],
            device_id=device, device_id_type=MESH,
        )
        for i, device in enumerate(others)
    ]
    for move in moves:
        move.start()

    loads[0].wait()
    queries[...] = query_stack(x_ref[...])

    def tile(which, raw, alpha, usable=None):
        stack, wh, wl = target_stack(raw, alpha, usable)
        targets[...] = stack.T
        both = jnp.concatenate([wh, wl], 0)

        def score(i):
            s = jnp.dot(
                targets[...], queries[:, i * CHUNK:(i + 1) * CHUNK], preferred_element_type=f32
            )
            scores[i % 2] = s
            return jnp.max(s, 0, keepdims=True)

        rounds = block // CHUNK
        top = score(0)
        for i in range(rounds):
            next_top = score(i + 1) if i + 1 < rounds else None
            e = jnp.exp2(scores[i % 2] - top)
            eh = e.astype(bf16)
            el = (e - eh.astype(f32)).astype(bf16)
            o = jnp.dot(both, eh, preferred_element_type=f32)
            o = o[:ROWS] + o[ROWS:] + jnp.dot(wh, el, preferred_element_type=f32)
            row = lax.broadcasted_iota(jnp.int32, o.shape, 0)
            o = jnp.where(row == ROWS - 1, top, o)
            for j in range(CHUNK // share):
                parts[which, i * (CHUNK // share) + j] = o[:, j * share:(j + 1) * share]
            top = next_top

        sends = []
        for k in range(1, peers):
            send = pltpu.make_async_remote_copy(
                src_ref=parts.at[which, lax.rem(c + k, peers)], dst_ref=got.at[which, k - 1],
                send_sem=part_send.at[which, k - 1], recv_sem=part_recv.at[which, k - 1],
                device_id=mates[k - 1], device_id_type=MESH,
            )
            send.start()
            sends.append(send)
        return sends

    def mean(which, sends, alpha):
        pieces = [parts[which, c]]
        for k, send in enumerate(sends):
            send.wait_recv()
            pieces.append(got[which, k])
        top = functools.reduce(jnp.maximum, [x[ROWS - 1:] for x in pieces])
        total = functools.reduce(jnp.add, [x * jnp.exp2(x[ROWS - 1:] - top) for x in pieces])
        return total[:30] / (total[30:31] * (2.0 * alpha))

    fit_alpha, bridge_alpha = (LOG2E / (2.0 * v) for v in (DATA_VAR, BRIDGE_VAR))
    loads[1].wait()
    cell = c * cells_ref.shape[1] + lax.broadcasted_iota(jnp.int32, (1, cells_ref.shape[1]), 1)
    sends = [tile(0, cells_ref[...], fit_alpha, cell < counts[t])]
    for i in (0, 1):
        moves[i].wait_recv()
        sends.append(tile(1 + i, near[i], bridge_alpha))
    loads[2].wait()
    means = [mean(i, sends[i], (fit_alpha, bridge_alpha, bridge_alpha)[i]) for i in range(3)]

    own = x_ref[:, pl.ds(pl.multiple_of(c * share, share), share)]
    has_prior = (t > 0).astype(f32)
    has_later = (t < times - 1).astype(f32)
    gradient = (own - means[0]) / DATA_VAR
    gradient = gradient + has_prior * (own - means[1]) / BRIDGE_VAR
    gradient = gradient + has_later * (own - means[2]) / BRIDGE_VAR
    d_out[0] = -gradient
    u_out[0] = (
        own - LANGEVIN_STRIDE * gradient
        + math.sqrt(2.0 * LANGEVIN_STRIDE * NOISE_LEVEL) * noise_ref[...]
    )
    for move in moves:
        move.wait_send()
    for group in sends:
        for send in group:
            send.wait_send()


def shards(sizes, particles, cell_points, cell_counts, brownian):
    _, dims, block = particles.shape
    cells = cell_points.shape[2]
    share = brownian.shape[2]
    peers = sizes[1]
    any_spec = pl.BlockSpec(memory_space=pl.ANY)
    vmem = pl.BlockSpec(memory_space=pltpu.VMEM)
    dma = pltpu.SemaphoreType.DMA
    return pl.pallas_call(
        functools.partial(kernel, sizes),
        out_shape=[jax.ShapeDtypeStruct((1, dims, share), f32)] * 2,
        in_specs=[pl.BlockSpec(memory_space=pltpu.SMEM), any_spec, any_spec, any_spec],
        out_specs=[vmem, vmem],
        scratch_shapes=[
            pltpu.VMEM((dims, block), f32),
            pltpu.VMEM((dims, cells), f32),
            pltpu.VMEM((dims, share), f32),
            pltpu.VMEM((2, dims, block), f32),
            pltpu.VMEM((6 * ROWS, block), bf16),
            pltpu.VMEM((max(block, cells), 6 * ROWS), bf16),
            pltpu.VMEM((2, max(block, cells), CHUNK), f32),
            pltpu.VMEM((3, peers, ROWS, share), f32),
            pltpu.VMEM((3, peers - 1, ROWS, share), f32),
            dma((3,)), dma((2,)), dma((2,)), dma((3, peers - 1)), dma((3, peers - 1)),
        ],
        compiler_params=pltpu.CompilerParams(
            collective_id=0, has_side_effects=True, vmem_limit_bytes=40 * 2**20
        ),
        name="langevin",
    )(cell_counts, particles, cell_points, brownian)


def solution(mesh):
    in_specs = (
        P("tm", None, "particle"),
        P("tm", None, "cell"),
        P(),
        P("tm", None, ("particle", "cell")),
    )
    out_specs = (P("tm", None, ("particle", "cell")), P("tm", None, ("particle", "cell")))
    sizes = (mesh.shape["tm"], mesh.shape["cell"])
    return jax.shard_map(
        functools.partial(shards, sizes),
        mesh=mesh, in_specs=in_specs, out_specs=out_specs, check_vma=False,
    )
```

time: 498 us -> 55.6 us (0.11)
  the two profiles are of different devices: /device:TPU:128 before, /device:TPU:16 now
where the time goes in v1:
time: 55.6 us; the launch traced here: 55.4 us
  Pallas kernels  51.2 us (92%)
  local copies, waits for them, and re-layouts  3.56 us (6%)
  between operations  0.67 us (1%)
    pallas_call x1, Pallas kernels, shards(): pl.pallas_call(functools.partial(kernel, sizes), out_shape=[jax.ShapeDtyp...  51.2 us
    unnamed x7, local copies, waits for them, and re-layouts  2.33 us
    pallas_call x2, local copies, waits for them, and re-layouts, shards(): pl.pallas_call(functools.partial(kernel, sizes), out_shape=[jax.ShapeDtyp...  1.23 us

profile of v1, /device:TPU:16, one launch (start us, length us, event | category | flops | bytes accessed | tf_op | source)
XLA Modules:
  0.0 55.4 jit_solution(16735457068484297620)
XLA Ops:
  0.6 0.7 %copy.8.noise_hbm = f32[1,30,128]{2,1,0:T(8,128)S(1)} copy(f32[1,30,128]{2,0,1:T(1,128)} %param.7) | data formatting | bytes 30720 | tf_op args[3]
  1.3 0.0 copy-start.1
  1.3 1.0 %copy.6.x_hbm = f32[1,30,1024]{2,1,0:T(8,128)S(1)} copy(f32[1,30,1024]{2,0,1:T(1,128)} %param.4) | data formatting | bytes 245760 | tf_op args[0]
  2.3 0.0 copy-done.1
  2.3 0.0 copy-start
  2.4 0.6 %copy-done = s32[8]{0:T(128)S(1)} copy-done((s32[8]{0:T(128)S(1)}, s32[8]{0:T(128)}, u32[]{:S(2)}) %copy-start) | copy-done | bytes 56
  3.0 51.2 %langevin.1 = (f32[1,30,128]{2,1,0:T(8,128)S(1)}, f32[1,30,128]{2,1,0:T(8,128)S(1)}) custom-call(s32[8]{0:T(128)S(1)} %copy-done, f32[1,30,1024]{2,1,0:T(8,128)S(1)} %copy.6.x_hbm, f32[1,30,1024]{2,1,0:T(8,128)S(1)} %copy.7.cells_hbm, f32[1,30,128]{2,1,0:T(8,128)S(1)} %copy.8.noise_hbm), custom_call_target="tpu_custom_call" | custom-call | tf_op jit(solution)/shard_map/langevin/pallas_call | solution.py:176
  54.2 0.6 %copy.9 = f32[1,30,128]{2,0,1:T(1,128)} copy(f32[1,30,128]{2,1,0:T(8,128)S(1)} %get-tuple-element.2) | data formatting | bytes 30720 | tf_op jit(solution)/shard_map/langevin/pallas_call | solution.py:176
  54.8 0.6 %copy.10 = f32[1,30,128]{2,0,1:T(1,128)} copy(f32[1,30,128]{2,1,0:T(8,128)S(1)} %get-tuple-element.3) | data formatting | bytes 30720 | tf_op jit(solution)/shard_map/langevin/pallas_call | solution.py:176
  (1 shorter events, 0.0 us)
Async XLA Ops:
  1.3 1.0 %copy-start.1 = (f32[1,30,1024]{2,0,1:T(1,128)S(1)}, f32[1,30,1024]{2,0,1:T(1,128)}, u32[]{:S(2)}) copy-start(f32[1,30,1024]{2,0,1:T(1,128)} %param.5) | copy-start | bytes 368644
  2.3 0.7 %copy-start = (s32[8]{0:T(128)S(1)}, s32[8]{0:T(128)}, u32[]{:S(2)}) copy-start(s32[8]{0:T(128)} %counts.1) | copy-start | bytes 100

commit v2 on v1

v2 whole, which is shorter than its diff:
```python
import functools
import math

import jax
import jax.numpy as jnp
from jax import lax
from jax.experimental import pallas as pl
from jax.experimental.pallas import tpu as pltpu
from jax.sharding import PartitionSpec as P

DATA_VAR = 2.0
BRIDGE_VAR = 1.5
LANGEVIN_STRIDE = 0.05
NOISE_LEVEL = 1.0
MASKED_SCORE = -1e30
LOG2E = math.log2(math.e)
MESH = pl.DeviceIdType.MESH
bf16, f32 = jnp.bfloat16, jnp.float32
ROWS = 32
CHUNK = 512


def split3(x):
    high = x.astype(bf16)
    rest = x - high.astype(f32)
    low = rest.astype(bf16)
    return high, low, (rest - low.astype(f32)).astype(bf16)


def query_stack(q):
    count = q.shape[1]
    ext = jnp.concatenate([q, jnp.ones((1, count), f32), jnp.zeros((1, count), f32)], 0)
    h, l, ll = split3(ext)
    return jnp.concatenate([h, h, l, l, h, ll], 0)


def target_stack(t, alpha, usable=None):
    count = t.shape[1]
    bias = -alpha * jnp.sum(t * t, 0, keepdims=True)
    if usable is not None:
        bias = jnp.where(usable, bias, MASKED_SCORE)
    ext = jnp.concatenate([t * (2.0 * alpha), bias, jnp.zeros((1, count), f32)], 0)
    h, l, ll = split3(ext)
    stack = jnp.concatenate([h, l, h, l, ll, h], 0)
    row = lax.broadcasted_iota(jnp.int32, ext.shape, 0)
    wh = jnp.where(row == 30, 1.0, h.astype(f32)).astype(bf16)
    wl = jnp.where(row == 30, 0.0, l.astype(f32)).astype(bf16)
    return stack.T, jnp.concatenate([wh, wl], 0)


def kernel(
    sizes,
    counts_hbm, x_hbm, cells_hbm, noise_hbm,
    d_out, u_out,
    counts, x_ref, cells_ref, noise_ref, near, slices, queries, targets, weights, scores, parts, got, done,
    in_sem, near_send, near_recv, slice_send, slice_recv, part_send, part_recv,
):
    times, blocks, peers = sizes
    t, p, c = (lax.axis_index(a) for a in ("tm", "particle", "cell"))
    share = noise_ref.shape[1]
    order = sorted(range(blocks), key=lambda k: -min(k, blocks - k))
    mine = pl.ds(pl.multiple_of(c * share, share), share)

    def local(src, dst, sem):
        copy = pltpu.make_async_copy(src, dst, sem)
        copy.start()
        return copy

    def remote(src, dst, send, recv, device):
        copy = pltpu.make_async_remote_copy(
            src_ref=src, dst_ref=dst, send_sem=send, recv_sem=recv,
            device_id=device, device_id_type=MESH,
        )
        copy.start()
        return copy

    load_x = local(x_hbm.at[:, 0, :], x_ref, in_sem.at[0])
    load_cells = local(cells_hbm.at[:, 0, :], cells_ref, in_sem.at[1])
    load_noise = local(noise_hbm.at[:, 0, :], noise_ref, in_sem.at[2])
    load_counts = local(counts_hbm, counts, in_sem.at[3])

    after, before = lax.rem(t + 1, times), lax.rem(t + times - 1, times)
    times_near = [(after, p, c), (before, p, c)]
    row_to = {k: (t, lax.rem(p + k, blocks), c) for k in range(1, blocks)}
    cell_to = {k: (t, p, lax.rem(c + k, peers)) for k in range(1, peers)}
    greeted = [row_to[k] for k in order if k] + times_near + list(cell_to.values())
    barrier = pltpu.get_barrier_semaphore()
    for device in greeted:
        pl.semaphore_signal(barrier, inc=1, device_id=device, device_id_type=MESH)
    pl.semaphore_wait(barrier, len(greeted))

    moves = [
        remote(x_hbm.at[:, 0, mine], slices.at[i], slice_send.at[i], slice_recv.at[i], row_to[k])
        for i, k in enumerate(order) if k
    ]
    moves += [
        remote(x_hbm.at[:, 0, :], near.at[i], near_send.at[i], near_recv.at[i], device)
        for i, device in enumerate(times_near)
    ]

    def score(which, queries_at, half, slot):
        s = jnp.dot(
            targets[which], queries[queries_at, :, half * CHUNK:(half + 1) * CHUNK],
            preferred_element_type=f32,
        )
        scores[slot] = s
        return jnp.max(s, 0, keepdims=True)

    def weigh(which, slot, top):
        e = jnp.exp2(scores[slot] - top)
        eh = e.astype(bf16)
        el = (e - eh.astype(f32)).astype(bf16)
        o = jnp.dot(weights[which], eh, preferred_element_type=f32)
        o = o[:ROWS] + o[ROWS:]
        o = o + jnp.dot(weights[which, :ROWS], el, preferred_element_type=f32)
        row = lax.broadcasted_iota(jnp.int32, o.shape, 0)
        return jnp.where(row == ROWS - 1, top, o)

    def prepare(which, raw, alpha, usable=None):
        targets[which], weights[which] = target_stack(raw, alpha, usable)

    fit_alpha, bridge_alpha = (LOG2E / (2.0 * v) for v in (DATA_VAR, BRIDGE_VAR))
    per = CHUNK // share
    halves = blocks // per

    def work(steps, after_step):
        top = score(*steps[0], 0)
        for i, step in enumerate(steps):
            next_top = score(*steps[i + 1], (i + 1) % 2) if i + 1 < len(steps) else None
            which, _, half = step
            o = weigh(which, i % 2, top)
            for j in range(per):
                parts[which, half * per + j] = o[:, j * share:(j + 1) * share]
            after_step(which, half)
            top = next_top

    load_x.wait()
    queries[0] = query_stack(x_ref[...])
    load_cells.wait()
    load_counts.wait()
    cell = c * cells_ref.shape[1] + lax.broadcasted_iota(jnp.int32, (1, cells_ref.shape[1]), 1)
    prepare(0, cells_ref[...], fit_alpha, cell < counts[t])
    work([(0, 0, half) for half in range(halves)], lambda which, half: None)
    sends = {}
    for k in range(1, peers):
        sends[0, k] = remote(
            parts.at[0, lax.rem(c + k, peers)], got.at[0, k],
            part_send.at[0, k], part_recv.at[0, k], cell_to[k],
        )

    own = x_ref[:, mine]
    for i, k in enumerate(order):
        if k:
            moves[i].wait_recv()
            queries[1, :, i * share:(i + 1) * share] = query_stack(slices[i])
        else:
            queries[1, :, i * share:(i + 1) * share] = query_stack(own)
    for i in (0, 1):
        moves[blocks - 1 + i].wait_recv()
        prepare(1 + i, near[i], bridge_alpha)

    def hand_back(which, half):
        for i in range(half * per, (half + 1) * per):
            if order[i]:
                sends[which, i] = remote(
                    parts.at[which, i], got.at[which, i],
                    part_send.at[which, i], part_recv.at[which, i], row_to[blocks - order[i]],
                )

    work([(which, 1, half) for half in range(halves) for which in (1, 2)], hand_back)

    def mean(which, home, alpha):
        pieces = [parts[which, home]]
        for (kind, i), send in sends.items():
            if kind == which:
                send.wait_recv()
                pieces.append(got[which, i])
        top = functools.reduce(jnp.maximum, [x[ROWS - 1:] for x in pieces])
        total = functools.reduce(jnp.add, [x * jnp.exp2(x[ROWS - 1:] - top) for x in pieces])
        return total[:30] / (total[30:31] * (2.0 * alpha))

    fit_mean = mean(0, c, fit_alpha)
    prior_mean = mean(1, blocks - 1, bridge_alpha)
    later_mean = mean(2, blocks - 1, bridge_alpha)
    has_prior = (t > 0).astype(f32)
    has_later = (t < times - 1).astype(f32)
    gradient = (own - fit_mean) / DATA_VAR
    gradient = gradient + has_prior * (own - prior_mean) / BRIDGE_VAR
    gradient = gradient + has_later * (own - later_mean) / BRIDGE_VAR
    load_noise.wait()
    done[0] = -gradient
    stores = [local(done.at[0], d_out.at[:, 0, :], in_sem.at[0])]
    done[1] = (
        own - LANGEVIN_STRIDE * gradient
        + math.sqrt(2.0 * LANGEVIN_STRIDE * NOISE_LEVEL) * noise_ref[...]
    )
    stores.append(local(done.at[1], u_out.at[:, 0, :], in_sem.at[1]))
    for copy in stores:
        copy.wait()
    for copy in moves + list(sends.values()):
        copy.wait_send()


def shards(sizes, particles, cell_points, cell_counts, brownian):
    _, dims, block = particles.shape
    cells = cell_points.shape[2]
    share = brownian.shape[2]
    _, blocks, peers = sizes
    assert blocks * share == block == cells and peers == blocks
    any_spec = pl.BlockSpec(memory_space=pl.ANY)
    dma = pltpu.SemaphoreType.DMA
    outs = pl.pallas_call(
        functools.partial(kernel, sizes),
        out_shape=[jax.ShapeDtypeStruct((dims, 1, share), f32)] * 2,
        in_specs=[any_spec] * 4,
        out_specs=[any_spec] * 2,
        scratch_shapes=[
            pltpu.SMEM(cell_counts.shape, jnp.int32),
            pltpu.VMEM((dims, block), f32),
            pltpu.VMEM((dims, cells), f32),
            pltpu.VMEM((dims, share), f32),
            pltpu.VMEM((2, dims, block), f32),
            pltpu.VMEM((blocks, dims, share), f32),
            pltpu.VMEM((2, 6 * ROWS, block), bf16),
            pltpu.VMEM((3, block, 6 * ROWS), bf16),
            pltpu.VMEM((3, 2 * ROWS, block), bf16),
            pltpu.VMEM((2, block, CHUNK), f32),
            pltpu.VMEM((3, blocks, ROWS, share), f32),
            pltpu.VMEM((3, blocks, ROWS, share), f32),
            pltpu.VMEM((2, dims, share), f32),
            dma((4,)), dma((2,)), dma((2,)), dma((blocks,)), dma((blocks,)),
            dma((3, blocks)), dma((3, blocks)),
        ],
        compiler_params=pltpu.CompilerParams(
            collective_id=0, has_side_effects=True, vmem_limit_bytes=62 * 2**20
        ),
        name="langevin",
    )(cell_counts, *(a.transpose(1, 0, 2) for a in (particles, cell_points, brownian)))
    return tuple(o.transpose(1, 0, 2) for o in outs)


def solution(mesh):
    in_specs = (
        P("tm", None, "particle"),
        P("tm", None, "cell"),
        P(),
        P("tm", None, ("particle", "cell")),
    )
    out_specs = (P("tm", None, ("particle", "cell")), P("tm", None, ("particle", "cell")))
    sizes = tuple(mesh.shape[a] for a in ("tm", "particle", "cell"))
    return jax.shard_map(
        functools.partial(shards, sizes),
        mesh=mesh, in_specs=in_specs, out_specs=out_specs, check_vma=False,
    )
```

time: 55.6 us -> 30.5 us (0.55)
  the two profiles are of different devices: /device:TPU:16 before, /device:TPU:8 now
where the time goes in v2:
time: 30.5 us; the launch traced here: 30.3 us
  Pallas kernels  27.7 us (91%)
  local copies, waits for them, and re-layouts  1.93 us (6%)
  between operations  0.65 us (2%)
    pallas_call x1, Pallas kernels, shards(): pl.pallas_call(functools.partial(kernel, sizes), out_shape=[jax.ShapeDtyp...  27.7 us
    unnamed x4, local copies, waits for them, and re-layouts  1.93 us

profile of v2, /device:TPU:8, one launch (start us, length us, event | category | flops | bytes accessed | tf_op | source)
XLA Modules:
  0.0 30.3 jit_solution(4440816507727486356)
XLA Ops:
  0.6 27.7 %langevin.1 = (f32[30,1,128]{2,1,0:T(1,128)}, f32[30,1,128]{2,1,0:T(1,128)}) custom-call(s32[8]{0:T(128)} %counts_hbm.1, f32[30,1,1024]{2,1,0:T(1,128)} %bitcast.5, f32[30,1,1024]{2,1,0:T(1,128)} %bitcast.6, f32[30,1,128]{2,1,0:T(1,128)} %bitcast.7), custom_call_target="tpu_custom_call" | custom-call | tf_op jit(solution)/shard_map/langevin/pallas_call | solution.py:212
  28.4 0.0 copy-start
  28.4 1.3 %copy.8 = f32[1,30,128]{2,0,1:T(1,128)} copy(f32[1,30,128]{2,0,1:T(1,128)} %bitcast.9) | data formatting | bytes 30720
  29.7 0.0 copy-done
  29.7 0.6 %copy.9 = f32[1,30,128]{2,0,1:T(1,128)} copy(f32[1,30,128]{2,0,1:T(1,128)S(1)} %bitcast.8) | data formatting | bytes 30720
Async XLA Ops:
  28.4 1.3 %copy-start = (f32[30,1,128]{2,1,0:T(1,128)S(1)}, f32[30,1,128]{2,1,0:T(1,128)}, u32[]{:S(2)}) copy-start(f32[30,1,128]{2,1,0:T(1,128)} %get-tuple-element.5) | copy-start | bytes 46084

commit v3 on v2

--- a/solution.py
+++ b/solution.py
@@ -51,9 +51,9 @@
 def kernel(
     sizes,
     counts_hbm, x_hbm, cells_hbm, noise_hbm,
-    d_out, u_out,
-    counts, x_ref, cells_ref, noise_ref, near, slices, queries, targets, weights, scores, parts, got, done,
-    in_sem, near_send, near_recv, slice_send, slice_recv, part_send, part_recv,
+    g_out, moved_out,
+    counts, x_ref, cells_ref, noise_ref, near, slices, queries, targets, weights, scores, parts, got, twin_sums, pair_sums,
+    in_sem, near_send, near_recv, slice_send, slice_recv, part_send, part_recv, twin_sem,
 ):
     times, blocks, peers = sizes
     t, p, c = (lax.axis_index(a) for a in ("tm", "particle", "cell"))
@@ -66,12 +66,13 @@
         copy.start()
         return copy
 
-    def remote(src, dst, send, recv, device):
+    def remote(src, dst, send, recv, device, start=True):
         copy = pltpu.make_async_remote_copy(
             src_ref=src, dst_ref=dst, send_sem=send, recv_sem=recv,
             device_id=device, device_id_type=MESH,
         )
-        copy.start()
+        if start:
+            copy.start()
         return copy
 
     load_x = local(x_hbm.at[:, 0, :], x_ref, in_sem.at[0])
@@ -81,21 +82,36 @@
 
     after, before = lax.rem(t + 1, times), lax.rem(t + times - 1, times)
     times_near = [(after, p, c), (before, p, c)]
+    has_prior, has_later = t > 0, t < times - 1
+    goes, comes = (has_later, has_prior), (has_prior, has_later)
     row_to = {k: (t, lax.rem(p + k, blocks), c) for k in range(1, blocks)}
-    cell_to = {k: (t, p, lax.rem(c + k, peers)) for k in range(1, peers)}
-    greeted = [row_to[k] for k in order if k] + times_near + list(cell_to.values())
+    pairs = peers // 2
+    x, side = lax.div(c, 2), lax.rem(c, 2)
+    twin = (t, p, 2 * x + 1 - side)
+    pair_to = {k: (t, p, 2 * lax.rem(x + k, pairs) + side) for k in range(1, pairs)}
+    greeted = [row_to[k] for k in order if k] + [twin] + list(pair_to.values())
     barrier = pltpu.get_barrier_semaphore()
+
+    def greet(device):
+        pl.semaphore_signal(barrier, inc=1, device_id=device, device_id_type=MESH)
+
     for device in greeted:
-        pl.semaphore_signal(barrier, inc=1, device_id=device, device_id_type=MESH)
-    pl.semaphore_wait(barrier, len(greeted))
-
-    moves = [
+        greet(device)
+    for go, device in zip(goes, times_near):
+        pl.when(go)(functools.partial(greet, device))
+    pl.semaphore_wait(
+        barrier, len(greeted) + has_prior.astype(jnp.int32) + has_later.astype(jnp.int32)
+    )
+
+    blocks_in = [
+        remote(x_hbm.at[:, 0, :], near.at[i], near_send.at[i], near_recv.at[i], device, False)
+        for i, device in enumerate(times_near)
+    ]
+    for go, copy in zip(goes, blocks_in):
+        pl.when(go)(copy.start)
+    slices_in = [
         remote(x_hbm.at[:, 0, mine], slices.at[i], slice_send.at[i], slice_recv.at[i], row_to[k])
         for i, k in enumerate(order) if k
-    ]
-    moves += [
-        remote(x_hbm.at[:, 0, :], near.at[i], near_send.at[i], near_recv.at[i], device)
-        for i, device in enumerate(times_near)
     ]
 
     def score(which, queries_at, half, slot):
@@ -130,7 +146,10 @@
             which, _, half = step
             o = weigh(which, i % 2, top)
             for j in range(per):
-                parts[which, half * per + j] = o[:, j * share:(j + 1) * share]
+                at = half * per + j
+                if which == 0:
+                    at = at % 2 * pairs + at // 2
+                parts[which, at] = o[:, j * share:(j + 1) * share]
             after_step(which, half)
             top = next_top
 
@@ -142,63 +161,91 @@
     prepare(0, cells_ref[...], fit_alpha, cell < counts[t])
     work([(0, 0, half) for half in range(halves)], lambda which, half: None)
     sends = {}
-    for k in range(1, peers):
-        sends[0, k] = remote(
-            parts.at[0, lax.rem(c + k, peers)], got.at[0, k],
-            part_send.at[0, k], part_recv.at[0, k], cell_to[k],
-        )
+    to_twin = remote(
+        parts.at[0, pl.ds((1 - side) * pairs, pairs)], twin_sums,
+        twin_sem.at[0], twin_sem.at[1], twin,
+    )
+
+    def merge(pieces):
+        top = functools.reduce(jnp.maximum, [q[ROWS - 1:] for q in pieces])
+        total = functools.reduce(jnp.add, [q * jnp.exp2(q[ROWS - 1:] - top) for q in pieces])
+        return top, total
+
+    def share_fit():
+        to_twin.wait_recv()
+        for j in range(pairs):
+            top, total = merge([parts[0, side * pairs + j], twin_sums[j]])
+            row = lax.broadcasted_iota(jnp.int32, total.shape, 0)
+            pair_sums[j] = jnp.where(row == ROWS - 1, top, total)
+        for k in range(1, pairs):
+            sends[0, k] = remote(
+                pair_sums.at[lax.rem(x + k, pairs)], got.at[0, k],
+                part_send.at[0, k], part_recv.at[0, k], pair_to[k],
+            )
 
     own = x_ref[:, mine]
-    for i, k in enumerate(order):
-        if k:
-            moves[i].wait_recv()
-            queries[1, :, i * share:(i + 1) * share] = query_stack(slices[i])
-        else:
-            queries[1, :, i * share:(i + 1) * share] = query_stack(own)
+    queries[1, :, (blocks - 1) * share:] = query_stack(own)
     for i in (0, 1):
-        moves[blocks - 1 + i].wait_recv()
+        pl.when(comes[i])(blocks_in[i].wait_recv)
+
+        @pl.when(jnp.logical_not(comes[i]))
+        def _():
+            near[i] = jnp.zeros(near.shape[1:], f32)
+
         prepare(1 + i, near[i], bridge_alpha)
+    for i, copy in enumerate(slices_in):
+        copy.wait_recv()
+        queries[1, :, i * share:(i + 1) * share] = query_stack(slices[i])
 
     def hand_back(which, half):
+        if (which, half) == (2, 0):
+            share_fit()
         for i in range(half * per, (half + 1) * per):
             if order[i]:
                 sends[which, i] = remote(
                     parts.at[which, i], got.at[which, i],
                     part_send.at[which, i], part_recv.at[which, i], row_to[blocks - order[i]],
+                    False,
                 )
 
+        @pl.when(comes[which - 1])
+        def _():
+            for i in range(half * per, (half + 1) * per):
+                if order[i]:
+                    sends[which, i].start()
+
     work([(which, 1, half) for half in range(halves) for which in (1, 2)], hand_back)
 
     def mean(which, home, alpha):
-        pieces = [parts[which, home]]
-        for (kind, i), send in sends.items():
+        pieces = [home] + [got[which, i] for kind, i in sends if kind == which]
+        _, total = merge(pieces)
+        return total[:30] / (total[30:31] * (2.0 * alpha))
+
+    def settle(which, wait):
+        for (kind, _), send in sends.items():
             if kind == which:
-                send.wait_recv()
-                pieces.append(got[which, i])
-        top = functools.reduce(jnp.maximum, [x[ROWS - 1:] for x in pieces])
-        total = functools.reduce(jnp.add, [x * jnp.exp2(x[ROWS - 1:] - top) for x in pieces])
-        return total[:30] / (total[30:31] * (2.0 * alpha))
-
-    fit_mean = mean(0, c, fit_alpha)
-    prior_mean = mean(1, blocks - 1, bridge_alpha)
-    later_mean = mean(2, blocks - 1, bridge_alpha)
-    has_prior = (t > 0).astype(f32)
-    has_later = (t < times - 1).astype(f32)
+                wait(send)
+
+    for wait in (lambda send: send.wait_recv(), lambda send: send.wait_send()):
+        settle(0, wait)
+        for i in (0, 1):
+            pl.when(comes[i])(functools.partial(settle, 1 + i, wait))
+    for go, copy in zip(goes, blocks_in):
+        pl.when(go)(copy.wait_send)
+    for copy in slices_in + [to_twin]:
+        copy.wait_send()
+
+    fit_mean = mean(0, pair_sums[x], fit_alpha)
+    prior_mean = mean(1, parts[1, blocks - 1], bridge_alpha)
+    later_mean = mean(2, parts[2, blocks - 1], bridge_alpha)
     gradient = (own - fit_mean) / DATA_VAR
-    gradient = gradient + has_prior * (own - prior_mean) / BRIDGE_VAR
-    gradient = gradient + has_later * (own - later_mean) / BRIDGE_VAR
+    gradient = gradient + jnp.where(has_prior, (own - prior_mean) / BRIDGE_VAR, 0.0)
+    gradient = gradient + jnp.where(has_later, (own - later_mean) / BRIDGE_VAR, 0.0)
     load_noise.wait()
-    done[0] = -gradient
-    stores = [local(done.at[0], d_out.at[:, 0, :], in_sem.at[0])]
-    done[1] = (
-        own - LANGEVIN_STRIDE * gradient
-        + math.sqrt(2.0 * LANGEVIN_STRIDE * NOISE_LEVEL) * noise_ref[...]
-    )
-    stores.append(local(done.at[1], u_out.at[:, 0, :], in_sem.at[1]))
-    for copy in stores:
-        copy.wait()
-    for copy in moves + list(sends.values()):
-        copy.wait_send()
+    g_out[:, 0, :] = gradient
+    moved_out[:, 0, :] = (
+        own + math.sqrt(2.0 * LANGEVIN_STRIDE * NOISE_LEVEL) * noise_ref[...]
+    )
 
 
 def shards(sizes, particles, cell_points, cell_counts, brownian):
@@ -209,11 +256,11 @@
     assert blocks * share == block == cells and peers == blocks
     any_spec = pl.BlockSpec(memory_space=pl.ANY)
     dma = pltpu.SemaphoreType.DMA
-    outs = pl.pallas_call(
+    gradient, moved = pl.pallas_call(
         functools.partial(kernel, sizes),
         out_shape=[jax.ShapeDtypeStruct((dims, 1, share), f32)] * 2,
         in_specs=[any_spec] * 4,
-        out_specs=[any_spec] * 2,
+        out_specs=[pl.BlockSpec(memory_space=pltpu.VMEM)] * 2,
         scratch_shapes=[
             pltpu.SMEM(cell_counts.shape, jnp.int32),
             pltpu.VMEM((dims, block), f32),
@@ -227,16 +274,18 @@
             pltpu.VMEM((2, block, CHUNK), f32),
             pltpu.VMEM((3, blocks, ROWS, share), f32),
             pltpu.VMEM((3, blocks, ROWS, share), f32),
-            pltpu.VMEM((2, dims, share), f32),
+            pltpu.VMEM((peers // 2, ROWS, share), f32),
+            pltpu.VMEM((peers // 2, ROWS, share), f32),
             dma((4,)), dma((2,)), dma((2,)), dma((blocks,)), dma((blocks,)),
-            dma((3, blocks)), dma((3, blocks)),
+            dma((3, blocks)), dma((3, blocks)), dma((2,)),
         ],
         compiler_params=pltpu.CompilerParams(
-            collective_id=0, has_side_effects=True, vmem_limit_bytes=62 * 2**20
+            collective_id=0, has_side_effects=True, vmem_limit_bytes=2**26 - 64 * 2**10
         ),
         name="langevin",
     )(cell_counts, *(a.transpose(1, 0, 2) for a in (particles, cell_points, brownian)))
-    return tuple(o.transpose(1, 0, 2) for o in outs)
+    gradient, moved = (a.transpose(1, 0, 2) for a in (gradient, moved))
+    return -gradient, moved - LANGEVIN_STRIDE * gradient
 
 
 def solution(mesh):

time: 30.5 us -> 26.7 us (0.88)
  the two profiles are of different devices: /device:TPU:8 before, /device:TPU:1 now
where the time goes in v3:
time: 26.7 us; the launch traced here: 26.5 us
  Pallas kernels  24.5 us (92%)
  other arithmetic  1.37 us (5%)
  between operations  0.64 us (2%)
    pallas_call x1, Pallas kernels, shards(): pl.pallas_call(functools.partial(kernel, sizes), out_shape=[jax.ShapeDtyp...  24.5 us
    sub x1, other arithmetic, shards(): return (-gradient, moved - LANGEVIN_STRIDE * gradient)  1.37 us

profile of v3, /device:TPU:1, one launch (start us, length us, event | category | flops | bytes accessed | tf_op | source)
XLA Modules:
  0.0 26.5 jit_solution(11085512692923589684)
XLA Ops:
  0.6 24.5 %langevin.1 = (f32[30,1,128]{2,1,0:T(1,128)}, f32[30,1,128]{2,1,0:T(1,128)}) custom-call(s32[8]{0:T(128)} %counts_hbm.1, f32[30,1,1024]{2,1,0:T(1,128)} %bitcast.7, f32[30,1,1024]{2,1,0:T(1,128)} %bitcast.8, f32[30,1,128]{2,1,0:T(1,128)} %bitcast.9), custom_call_target="tpu_custom_call" | custom-call | tf_op jit(solution)/shard_map/langevin/pallas_call | solution.py:259
  25.1 1.4 %subtract_bitcast_fusion = (f32[1,30,128]{2,0,1:T(1,128)}, f32[1,30,128]{2,0,1:T(1,128)}) fusion(f32[30,1,128]{2,1,0:T(1,128)} %get-tuple-element.5, f32[30,1,128]{2,1,0:T(1,128)} %get-tuple-element.4), kind=kLoop, calls=%fused_computation | loop fusion | flops 11520 | bytes 61440 | tf_op jit(solution)/shard_map/sub | solution.py:288

commit v4 on v3

--- a/solution.py
+++ b/solution.py
@@ -17,7 +17,7 @@
 MESH = pl.DeviceIdType.MESH
 bf16, f32 = jnp.bfloat16, jnp.float32
 ROWS = 32
-CHUNK = 512
+CHUNK = 256
 
 
 def split3(x):
@@ -75,11 +75,6 @@
             copy.start()
         return copy
 
-    load_x = local(x_hbm.at[:, 0, :], x_ref, in_sem.at[0])
-    load_cells = local(cells_hbm.at[:, 0, :], cells_ref, in_sem.at[1])
-    load_noise = local(noise_hbm.at[:, 0, :], noise_ref, in_sem.at[2])
-    load_counts = local(counts_hbm, counts, in_sem.at[3])
-
     after, before = lax.rem(t + 1, times), lax.rem(t + times - 1, times)
     times_near = [(after, p, c), (before, p, c)]
     has_prior, has_later = t > 0, t < times - 1
@@ -99,6 +94,10 @@
         greet(device)
     for go, device in zip(goes, times_near):
         pl.when(go)(functools.partial(greet, device))
+    load_x = local(x_hbm.at[:, 0, :], x_ref, in_sem.at[0])
+    load_cells = local(cells_hbm.at[:, 0, :], cells_ref, in_sem.at[1])
+    load_noise = local(noise_hbm.at[:, 0, :], noise_ref, in_sem.at[2])
+    load_counts = local(counts_hbm, counts, in_sem.at[3])
     pl.semaphore_wait(
         barrier, len(greeted) + has_prior.astype(jnp.int32) + has_later.astype(jnp.int32)
     )
@@ -115,6 +114,8 @@
     ]
 
     def score(which, queries_at, half, slot):
+        if which:
+            ready(which, half)
         s = jnp.dot(
             targets[which], queries[queries_at, :, half * CHUNK:(half + 1) * CHUNK],
             preferred_element_type=f32,
@@ -185,17 +186,21 @@
 
     own = x_ref[:, mine]
     queries[1, :, (blocks - 1) * share:] = query_stack(own)
-    for i in (0, 1):
-        pl.when(comes[i])(blocks_in[i].wait_recv)
-
-        @pl.when(jnp.logical_not(comes[i]))
-        def _():
-            near[i] = jnp.zeros(near.shape[1:], f32)
-
-        prepare(1 + i, near[i], bridge_alpha)
-    for i, copy in enumerate(slices_in):
-        copy.wait_recv()
-        queries[1, :, i * share:(i + 1) * share] = query_stack(slices[i])
+
+    def ready(which, half):
+        if half == 0:
+            i = which - 1
+            pl.when(comes[i])(blocks_in[i].wait_recv)
+
+            @pl.when(jnp.logical_not(comes[i]))
+            def _():
+                near[i] = jnp.zeros(near.shape[1:], f32)
+
+            prepare(which, near[i], bridge_alpha)
+        if which == 1:
+            for i in range(half * per, min((half + 1) * per, blocks - 1)):
+                slices_in[i].wait_recv()
+                queries[1, :, i * share:(i + 1) * share] = query_stack(slices[i])
 
     def hand_back(which, half):
         if (which, half) == (2, 0):
@@ -226,15 +231,12 @@
             if kind == which:
                 wait(send)
 
-    for wait in (lambda send: send.wait_recv(), lambda send: send.wait_send()):
+    def settle_all(wait):
         settle(0, wait)
         for i in (0, 1):
             pl.when(comes[i])(functools.partial(settle, 1 + i, wait))
-    for go, copy in zip(goes, blocks_in):
-        pl.when(go)(copy.wait_send)
-    for copy in slices_in + [to_twin]:
-        copy.wait_send()
-
+
+    settle_all(lambda send: send.wait_recv())
     fit_mean = mean(0, pair_sums[x], fit_alpha)
     prior_mean = mean(1, parts[1, blocks - 1], bridge_alpha)
     later_mean = mean(2, parts[2, blocks - 1], bridge_alpha)
@@ -246,6 +248,11 @@
     moved_out[:, 0, :] = (
         own + math.sqrt(2.0 * LANGEVIN_STRIDE * NOISE_LEVEL) * noise_ref[...]
     )
+    settle_all(lambda send: send.wait_send())
+    for go, copy in zip(goes, blocks_in):
+        pl.when(go)(copy.wait_send)
+    for copy in slices_in + [to_twin]:
+        copy.wait_send()
 
 
 def shards(sizes, particles, cell_points, cell_counts, brownian):

time: 26.7 us -> 25.9 us (0.970)
  the two profiles are of different devices: /device:TPU:1 before, /device:TPU:193 now
where the time goes in v4:
time: 25.9 us; the launch traced here: 25.7 us
  Pallas kernels  23.6 us (91%)
  other arithmetic  1.37 us (5%)
  between operations  0.64 us (2%)
    pallas_call x1, Pallas kernels, shards(): pl.pallas_call(functools.partial(kernel, sizes), out_shape=[jax.ShapeDtyp...  23.6 us
    sub x1, other arithmetic, shards(): return (-gradient, moved - LANGEVIN_STRIDE * gradient)  1.37 us

profile of v4, /device:TPU:193, one launch (start us, length us, event | category | flops | bytes accessed | tf_op | source)
XLA Modules:
  0.0 25.7 jit_solution(15274972486716673080)
XLA Ops:
  0.6 23.6 %langevin.1 = (f32[30,1,128]{2,1,0:T(1,128)}, f32[30,1,128]{2,1,0:T(1,128)}) custom-call(s32[8]{0:T(128)} %counts_hbm.1, f32[30,1,1024]{2,1,0:T(1,128)} %bitcast.7, f32[30,1,1024]{2,1,0:T(1,128)} %bitcast.8, f32[30,1,128]{2,1,0:T(1,128)} %bitcast.9), custom_call_target="tpu_custom_call" | custom-call | tf_op jit(solution)/shard_map/langevin/pallas_call | solution.py:266
  24.3 1.4 %subtract_bitcast_fusion = (f32[1,30,128]{2,0,1:T(1,128)}, f32[1,30,128]{2,0,1:T(1,128)}) fusion(f32[30,1,128]{2,1,0:T(1,128)} %get-tuple-element.5, f32[30,1,128]{2,1,0:T(1,128)} %get-tuple-element.4), kind=kLoop, calls=%fused_computation | loop fusion | flops 11520 | bytes 61440 | tf_op jit(solution)/shard_map/sub | solution.py:295

commit v5 on v4

--- a/solution.py
+++ b/solution.py
@@ -90,10 +90,12 @@
     def greet(device):
         pl.semaphore_signal(barrier, inc=1, device_id=device, device_id_type=MESH)
 
-    for device in greeted:
+    for device in greeted[:2]:
         greet(device)
     for go, device in zip(goes, times_near):
         pl.when(go)(functools.partial(greet, device))
+    for device in greeted[2:]:
+        greet(device)
     load_x = local(x_hbm.at[:, 0, :], x_ref, in_sem.at[0])
     load_cells = local(cells_hbm.at[:, 0, :], cells_ref, in_sem.at[1])
     load_noise = local(noise_hbm.at[:, 0, :], noise_ref, in_sem.at[2])
@@ -106,12 +108,13 @@
         remote(x_hbm.at[:, 0, :], near.at[i], near_send.at[i], near_recv.at[i], device, False)
         for i, device in enumerate(times_near)
     ]
-    for go, copy in zip(goes, blocks_in):
-        pl.when(go)(copy.start)
+    pl.when(goes[0])(blocks_in[0].start)
     slices_in = [
         remote(x_hbm.at[:, 0, mine], slices.at[i], slice_send.at[i], slice_recv.at[i], row_to[k])
         for i, k in enumerate(order) if k
     ]
+
+    pl.when(goes[1])(blocks_in[1].start)
 
     def score(which, queries_at, half, slot):
         if which:
@@ -219,7 +222,7 @@
                 if order[i]:
                     sends[which, i].start()
 
-    work([(which, 1, half) for half in range(halves) for which in (1, 2)], hand_back)
+    work([(which, 1, half) for which in (1, 2) for half in range(halves)], hand_back)
 
     def mean(which, home, alpha):
         pieces = [home] + [got[which, i] for kind, i in sends if kind == which]
@@ -236,9 +239,12 @@
         for i in (0, 1):
             pl.when(comes[i])(functools.partial(settle, 1 + i, wait))
 
-    settle_all(lambda send: send.wait_recv())
+    arrive = lambda send: send.wait_recv()
+    settle(0, arrive)
     fit_mean = mean(0, pair_sums[x], fit_alpha)
+    pl.when(comes[0])(functools.partial(settle, 1, arrive))
     prior_mean = mean(1, parts[1, blocks - 1], bridge_alpha)
+    pl.when(comes[1])(functools.partial(settle, 2, arrive))
     later_mean = mean(2, parts[2, blocks - 1], bridge_alpha)
     gradient = (own - fit_mean) / DATA_VAR
     gradient = gradient + jnp.where(has_prior, (own - prior_mean) / BRIDGE_VAR, 0.0)

time: 25.9 us -> 25.3 us (0.977)
  the two profiles are of different devices: /device:TPU:193 before, /device:TPU:135 now
where the time goes in v5:
time: 25.3 us; the launch traced here: 25.1 us
  Pallas kernels  23.1 us (91%)
  other arithmetic  1.37 us (5%)
  between operations  0.64 us (3%)
    pallas_call x1, Pallas kernels, shards(): pl.pallas_call(functools.partial(kernel, sizes), out_shape=[jax.ShapeDtyp...  23.1 us
    sub x1, other arithmetic, shards(): return (-gradient, moved - LANGEVIN_STRIDE * gradient)  1.37 us

profile of v5, /device:TPU:135, one launch (start us, length us, event | category | flops | bytes accessed | tf_op | source)
XLA Modules:
  0.0 25.1 jit_solution(4230609103861829054)
XLA Ops:
  0.6 23.1 %langevin.1 = (f32[30,1,128]{2,1,0:T(1,128)}, f32[30,1,128]{2,1,0:T(1,128)}) custom-call(s32[8]{0:T(128)} %counts_hbm.1, f32[30,1,1024]{2,1,0:T(1,128)} %bitcast.7, f32[30,1,1024]{2,1,0:T(1,128)} %bitcast.8, f32[30,1,128]{2,1,0:T(1,128)} %bitcast.9), custom_call_target="tpu_custom_call" | custom-call | tf_op jit(solution)/shard_map/langevin/pallas_call | solution.py:272
  23.7 1.4 %subtract_bitcast_fusion = (f32[1,30,128]{2,0,1:T(1,128)}, f32[1,30,128]{2,0,1:T(1,128)}) fusion(f32[30,1,128]{2,1,0:T(1,128)} %get-tuple-element.5, f32[30,1,128]{2,1,0:T(1,128)} %get-tuple-element.4), kind=kLoop, calls=%fused_computation | loop fusion | flops 11520 | bytes 61440 | tf_op jit(solution)/shard_map/sub | solution.py:301

commit v6 on v5

--- a/solution.py
+++ b/solution.py
@@ -52,7 +52,7 @@
     sizes,
     counts_hbm, x_hbm, cells_hbm, noise_hbm,
     g_out, moved_out,
-    counts, x_ref, cells_ref, noise_ref, near, slices, queries, targets, weights, scores, parts, got, twin_sums, pair_sums,
+    counts, x_ref, cells_ref, noise_ref, near, slices, queries, targets, weights, scores, parts, got, side_sums, pair_sums,
     in_sem, near_send, near_recv, slice_send, slice_recv, part_send, part_recv, twin_sem,
 ):
     times, blocks, peers = sizes
@@ -151,8 +151,6 @@
             o = weigh(which, i % 2, top)
             for j in range(per):
                 at = half * per + j
-                if which == 0:
-                    at = at % 2 * pairs + at // 2
                 parts[which, at] = o[:, j * share:(j + 1) * share]
             after_step(which, half)
             top = next_top
@@ -165,10 +163,13 @@
     prepare(0, cells_ref[...], fit_alpha, cell < counts[t])
     work([(0, 0, half) for half in range(halves)], lambda which, half: None)
     sends = {}
-    to_twin = remote(
-        parts.at[0, pl.ds((1 - side) * pairs, pairs)], twin_sums,
-        twin_sem.at[0], twin_sem.at[1], twin,
-    )
+    to_pairs = [
+        remote(
+            parts.at[0, pl.ds(2 * lax.rem(x + k, pairs), 2)], side_sums.at[k - 1],
+            part_send.at[0, k], part_recv.at[0, k], pair_to[k],
+        )
+        for k in range(1, pairs)
+    ]
 
     def merge(pieces):
         top = functools.reduce(jnp.maximum, [q[ROWS - 1:] for q in pieces])
@@ -176,16 +177,15 @@
         return top, total
 
     def share_fit():
-        to_twin.wait_recv()
-        for j in range(pairs):
-            top, total = merge([parts[0, side * pairs + j], twin_sums[j]])
+        for copy in to_pairs:
+            copy.wait_recv()
+        for j in range(2):
+            top, total = merge([parts[0, 2 * x + j]] + [side_sums[k, j] for k in range(pairs - 1)])
             row = lax.broadcasted_iota(jnp.int32, total.shape, 0)
             pair_sums[j] = jnp.where(row == ROWS - 1, top, total)
-        for k in range(1, pairs):
-            sends[0, k] = remote(
-                pair_sums.at[lax.rem(x + k, pairs)], got.at[0, k],
-                part_send.at[0, k], part_recv.at[0, k], pair_to[k],
-            )
+        sends[0, 0] = remote(
+            pair_sums.at[1 - side], got.at[0, 0], twin_sem.at[0], twin_sem.at[1], twin
+        )
 
     own = x_ref[:, mine]
     queries[1, :, (blocks - 1) * share:] = query_stack(own)
@@ -241,7 +241,7 @@
 
     arrive = lambda send: send.wait_recv()
     settle(0, arrive)
-    fit_mean = mean(0, pair_sums[x], fit_alpha)
+    fit_mean = mean(0, pair_sums[side], fit_alpha)
     pl.when(comes[0])(functools.partial(settle, 1, arrive))
     prior_mean = mean(1, parts[1, blocks - 1], bridge_alpha)
     pl.when(comes[1])(functools.partial(settle, 2, arrive))
@@ -257,7 +257,7 @@
     settle_all(lambda send: send.wait_send())
     for go, copy in zip(goes, blocks_in):
         pl.when(go)(copy.wait_send)
-    for copy in slices_in + [to_twin]:
+    for copy in slices_in + to_pairs:
         copy.wait_send()
 
 
@@ -287,8 +287,8 @@
             pltpu.VMEM((2, block, CHUNK), f32),
             pltpu.VMEM((3, blocks, ROWS, share), f32),
             pltpu.VMEM((3, blocks, ROWS, share), f32),
-            pltpu.VMEM((peers // 2, ROWS, share), f32),
-            pltpu.VMEM((peers // 2, ROWS, share), f32),
+            pltpu.VMEM((peers // 2 - 1, 2, ROWS, share), f32),
+            pltpu.VMEM((2, ROWS, share), f32),
             dma((4,)), dma((2,)), dma((2,)), dma((blocks,)), dma((blocks,)),
             dma((3, blocks)), dma((3, blocks)), dma((2,)),
         ],

time: 25.3 us -> 25.3 us (level)
  no operation moved by 1% of the time
where the time goes in v6:
time: 25.3 us; the launch traced here: 25.1 us
  Pallas kernels  23.1 us (91%)
  other arithmetic  1.37 us (5%)
  between operations  0.64 us (3%)
    pallas_call x1, Pallas kernels, shards(): pl.pallas_call(functools.partial(kernel, sizes), out_shape=[jax.ShapeDtyp...  23.1 us
    sub x1, other arithmetic, shards(): return (-gradient, moved - LANGEVIN_STRIDE * gradient)  1.37 us

profile of v6, /device:TPU:135, one launch (start us, length us, event | category | flops | bytes accessed | tf_op | source)
XLA Modules:
  0.0 25.1 jit_solution(2022890499436537158)
XLA Ops:
  0.6 23.1 %langevin.1 = (f32[30,1,128]{2,1,0:T(1,128)}, f32[30,1,128]{2,1,0:T(1,128)}) custom-call(s32[8]{0:T(128)} %counts_hbm.1, f32[30,1,1024]{2,1,0:T(1,128)} %bitcast.7, f32[30,1,1024]{2,1,0:T(1,128)} %bitcast.8, f32[30,1,128]{2,1,0:T(1,128)} %bitcast.9), custom_call_target="tpu_custom_call" | custom-call | tf_op jit(solution)/shard_map/langevin/pallas_call | solution.py:272
  23.7 1.4 %subtract_bitcast_fusion = (f32[1,30,128]{2,0,1:T(1,128)}, f32[1,30,128]{2,0,1:T(1,128)}) fusion(f32[30,1,128]{2,1,0:T(1,128)} %get-tuple-element.5, f32[30,1,128]{2,1,0:T(1,128)} %get-tuple-element.4), kind=kLoop, calls=%fused_computation | loop fusion | flops 11520 | bytes 61440 | tf_op jit(solution)/shard_map/sub | solution.py:301

commit v7 on v6

--- a/solution.py
+++ b/solution.py
@@ -117,8 +117,10 @@
     pl.when(goes[1])(blocks_in[1].start)
 
     def score(which, queries_at, half, slot):
-        if which:
-            ready(which, half)
+        if which == 1:
+            ready(1, half)
+            if half == halves - 1:
+                ready(2, 0)
         s = jnp.dot(
             targets[which], queries[queries_at, :, half * CHUNK:(half + 1) * CHUNK],
             preferred_element_type=f32,

time: 25.3 us -> 25.2 us (level)
  the two profiles are of different devices: /device:TPU:135 before, /device:TPU:129 now
where the time goes in v7:
time: 25.2 us; the launch traced here: 25 us
  Pallas kernels  23 us (91%)
  other arithmetic  1.37 us (5%)
  between operations  0.64 us (3%)
    pallas_call x1, Pallas kernels, shards(): pl.pallas_call(functools.partial(kernel, sizes), out_shape=[jax.ShapeDtyp...  23 us
    sub x1, other arithmetic, shards(): return (-gradient, moved - LANGEVIN_STRIDE * gradient)  1.37 us

profile of v7, /device:TPU:129, one launch (start us, length us, event | category | flops | bytes accessed | tf_op | source)
XLA Modules:
  0.0 25.0 jit_solution(17678546853266592728)
XLA Ops:
  0.6 23.0 %langevin.1 = (f32[30,1,128]{2,1,0:T(1,128)}, f32[30,1,128]{2,1,0:T(1,128)}) custom-call(s32[8]{0:T(128)} %counts_hbm.1, f32[30,1,1024]{2,1,0:T(1,128)} %bitcast.7, f32[30,1,1024]{2,1,0:T(1,128)} %bitcast.8, f32[30,1,128]{2,1,0:T(1,128)} %bitcast.9), custom_call_target="tpu_custom_call" | custom-call | tf_op jit(solution)/shard_map/langevin/pallas_call | solution.py:274
  23.7 1.4 %subtract_bitcast_fusion = (f32[1,30,128]{2,0,1:T(1,128)}, f32[1,30,128]{2,0,1:T(1,128)}) fusion(f32[30,1,128]{2,1,0:T(1,128)} %get-tuple-element.5, f32[30,1,128]{2,1,0:T(1,128)} %get-tuple-element.4), kind=kLoop, calls=%fused_computation | loop fusion | flops 11520 | bytes 61440 | tf_op jit(solution)/shard_map/sub | solution.py:303
